TPU v7x, 32 devices: a whole 2x2x4 slice. The times are simulated.
32 devices in a mesh: grain: 4 (over z), row: 8 (over y, x, core).
Axes of the slice: x: 2, y: 2, z: 4, core: 2. Of those that a mesh axis runs over, the one named last changes fastest.
Arguments:
- order_params: float32 [64, 4, 1024, 1024], P('grain', None, 'row'), may hold values from 0 to 0.5
- eigen_weight: float32 [64], P('grain'), may hold values from -1 to 1
- green: float32 [1024, 1024], replicated, may hold values from 0.25 to 2
Outputs:
- updated: float32 [64, 4, 1024, 1024], P('grain', None, 'row')
- potential: float32 [4, 1024, 1024], P(None, 'row')
All inputs are finite; a program needn't handle non-finite values.
Results may differ from a plain program's by a relative error of at most 0.00016.
Values sent between devices are 32-bit elements; how exact they have to be, the bound alone decides.
A program may use at most 256 MiB of HBM per device.

v0:
```python
import math

import jax
import jax.numpy as jnp
from jax import lax
from jax.sharding import PartitionSpec as P

STEPS = 3


time_step = 0.1
alpha_coef = 1.0
beta_coef = 1.0
gamma_coef = 0.25
kappa_coef = 1.0
elastic_coef = 2.0


def with_halo(x, sides, width):
    for axis, dim in sides:
        devices, length = (lax.axis_size(axis), x.shape[dim])
        up = [(i, (i + 1) % devices) for i in range(devices)]
        down = [(j, i) for i, j in up]
        last = lax.slice_in_dim(x, length - width, length, axis=dim)
        leading = lax.slice_in_dim(x, 0, width, axis=dim)
        before = lax.ppermute(last, axis, up)
        after = lax.ppermute(leading, axis, down)
        x = jnp.concatenate([before, x, after], axis=dim)
    return x


def advance(extended):
    center = extended[:, :, 1:-1]
    totals = lax.psum(jnp.sum(center * center, axis=0), "grain")
    laplacian = (
        extended[:, :, 2:]
        + extended[:, :, :-2]
        + jnp.roll(center, 1, 3)
        + jnp.roll(center, -1, 3)
        - 4.0 * center
    )
    others = totals[None] - center * center
    chemical = (
        -alpha_coef * center
        + beta_coef * center**3
        + 2.0 * gamma_coef * center * others
        - kappa_coef * laplacian
    )
    return center - time_step * chemical


def phase_tables(freqs, places, length):
    product = freqs[:, None] * places[None, :] % length
    angle = product.astype(jnp.float32) * (2.0 * math.pi / length)
    return (jnp.cos(angle), jnp.sin(angle))


def forward_rows(matrix, values):
    return jnp.einsum(
        "kq,pqc->pkc",
        matrix,
        values,
        precision=lax.Precision.HIGHEST,
        preferred_element_type=jnp.float32,
    )


def backward_rows(matrix, values):
    return jnp.einsum(
        "kq,pkc->pqc",
        matrix,
        values,
        precision=lax.Precision.HIGHEST,
        preferred_element_type=jnp.float32,
    )


def inner_transform(piece, green, row_index, col_start):
    length = piece.shape[1]
    columns = piece.shape[3]
    freqs = jnp.arange(length, dtype=jnp.int32)
    cosine, sine = phase_tables(freqs, row_index, length)
    real_part = piece[:, :, 0]
    imag_part = piece[:, :, 1]
    fwd_real = forward_rows(cosine, real_part) + forward_rows(sine, imag_part)
    fwd_imag = forward_rows(cosine, imag_part) - forward_rows(sine, real_part)
    local_green = lax.dynamic_slice_in_dim(green, col_start, columns, 1)
    scaled_real = fwd_real * local_green[None]
    scaled_imag = fwd_imag * local_green[None]
    inv_real = backward_rows(cosine, scaled_real) - backward_rows(sine, scaled_imag)
    inv_imag = backward_rows(cosine, scaled_imag) + backward_rows(sine, scaled_real)
    return jnp.stack([inv_real, inv_imag], axis=2)


def row_forward(strain, cosine, sine):
    planes, rows_here, length = strain.shape
    flat = strain.reshape(planes * rows_here, length)
    table = jnp.concatenate([cosine, -sine], axis=1)
    result = jnp.dot(
        flat, table, precision=lax.Precision.HIGHEST, preferred_element_type=jnp.float32
    )
    return result.reshape(planes, rows_here, 2, length)


def row_backward(mixed, cosine, sine):
    planes, rows_here, pair, length = mixed.shape
    flat = mixed.reshape(planes * rows_here, pair * length)
    table = jnp.concatenate([cosine, -sine], axis=0)
    result = jnp.dot(
        flat, table, precision=lax.Precision.HIGHEST, preferred_element_type=jnp.float32
    )
    return (result * (1.0 / (length * length))).reshape(planes, rows_here, length)


def local(order_params, eigen_weight, green):
    order = order_params
    for repeat in range(STEPS):
        extended = with_halo(order, (("row", 2),), 1)
        order = advance(extended)
    strain = jnp.sum(eigen_weight[:, None, None, None] * order * order, axis=0)
    length = order.shape[3]
    grains = lax.axis_size("grain")
    row_count = lax.axis_size("row")
    positions = jnp.arange(length, dtype=jnp.int32)
    cosine, sine = phase_tables(positions, positions, length)
    strain = lax.psum_scatter(strain, "grain", scatter_dimension=1, tiled=True)
    block = strain.shape[1]
    full_rows = block * grains
    source = positions // block
    row_index = source % row_count * full_rows + source // row_count * block + positions % block
    col_start = (lax.axis_index("grain") * row_count + lax.axis_index("row")) * (
        length // (grains * row_count)
    )
    forward = row_forward(strain, cosine, sine)
    mixed_piece = inner_transform(
        lax.all_to_all(forward, ("grain", "row"), split_axis=3, concat_axis=1, tiled=True),
        green,
        row_index,
        col_start,
    )
    mixed = lax.all_to_all(mixed_piece, ("grain", "row"), split_axis=1, concat_axis=3, tiled=True)
    potential = row_backward(mixed, cosine, sine)
    potential = lax.all_gather(potential, "grain", axis=1, tiled=True)
    factor = time_step * 2.0 * elastic_coef
    updated = order - factor * eigen_weight[:, None, None, None] * order * potential[None]
    return (updated, potential)


def solution(mesh):
    return jax.shard_map(
        local,
        mesh=mesh,
        in_specs=(P("grain", None, "row", None), P("grain"), P()),
        out_specs=(P("grain", None, "row", None), P(None, "row", None)),
        check_vma=False,
    )
```

profile of v0, /device:TPU:0, one launch (start us, length us, event | category | flops | bytes accessed | tf_op | source)
XLA Modules:
  0.0 959.2 jit_solution(15638896293911631519)
XLA Ops:
  7.2 35.1 %multiply_reduce_fusion.2 = (f32[4,128,1024]{2,1,0:T(8,128)}, f32[16,4,128,1024]{3,0,2,1:T(8,128)S(1)}) fusion(f32[16,4,128,1024]{3,2,1,0:T(8,128)} %param.3), kind=kLoop, calls=%fused_computation.35 | loop fusion | flops 16252928 | bytes 69206016 | tf_op jit(solution)/shard_map/reduce_sum | solution.py:34
  42.3 11.7 %copy-done = f32[16,4,128,1024]{3,0,2,1:T(8,128)} copy-done((f32[16,4,128,1024]{3,0,2,1:T(8,128)}, f32[16,4,128,1024]{3,0,2,1:T(8,128)S(1)}, u32[]{:S(2)}) %copy-start) | copy-done | bytes 33554456
  57.8 46.0 %fusion.162 = (f32[16,4,128,1023]{3,0,2,1:T(8,128)}, f32[16,4,128,1023]{3,0,2,1:T(8,128)}) fusion(f32[16,4,128,1024]{3,0,2,1:T(8,128)} %copy-done), kind=kLoop, calls=%fused_computation.167 | loop fusion | bytes 134086656 | tf_op jit(solution)/shard_map/jit(_roll_static)/slice | solution.py:38
  103.8 8.2 fusion.161
  111.9 33.6 %all-reduce.4.cloned.1.call-done = f32[4,128,1024]{2,1,0:T(8,128)} async-done(((f32[4,128,1024]{2,1,0:T(8,128)}), f32[4,128,1024]{2,1,0:T(8,128)}) %all-reduce.4.cloned.1.call-update) | async-done | bytes 2097168 | tf_op jit(solution)/shard_map/psum | solution.py:34
  145.5 70.4 %multiply_reduce_fusion.1 = (f32[4,128,1024]{2,1,0:T(8,128)}, f32[16,4,128,1024]{3,0,2,1:T(8,128)}) fusion(f32[16,4,128,1024]{3,0,2,1:T(8,128)} %copy-done, f32[16,4,128,1]{3,0,2,1:T(8,128)} %get-tuple-element.27, f32[16,4,128,1023]{3,0,2,1:T(8,128)} %get-tuple-element.29, f32[16,4,128,1023]{3,0,2,1:T(8,128)} %get-tuple-element.28, ...), kind=kLoop, calls=%fused_computation.34 | loop fusion | flops 175636480 | bytes 138936320 | tf_op jit(solution)/shard_map/reduce_sum | solution.py:34
  216.0 45.9 %fusion.159 = (f32[16,4,128,1023]{3,0,2,1:T(8,128)}, f32[16,4,128,1023]{3,0,2,1:T(8,128)}) fusion(f32[16,4,128,1024]{3,0,2,1:T(8,128)} %get-tuple-element.9), kind=kLoop, calls=%fused_computation.164 | loop fusion | bytes 134086656 | tf_op jit(solution)/shard_map/jit(_roll_static)/slice | solution.py:38
  265.2 8.2 fusion.158
  273.4 28.2 %all-reduce.6.cloned.1.call-done = f32[4,128,1024]{2,1,0:T(8,128)} async-done(((f32[4,128,1024]{2,1,0:T(8,128)}), f32[4,128,1024]{2,1,0:T(8,128)}) %all-reduce.6.cloned.1.call-update) | async-done | bytes 2097168 | tf_op jit(solution)/shard_map/psum | solution.py:34
  301.6 70.1 %multiply_reduce_fusion = (f32[4,128,1024]{2,1,0:T(8,128)}, f32[16,4,128,1024]{3,0,2,1:T(8,128)}) fusion(f32[16,4,128,1024]{3,0,2,1:T(8,128)} %get-tuple-element.9, f32[16,4,128,1]{3,0,2,1:T(8,128)} %get-tuple-element.19, f32[16,4,128,1023]{3,0,2,1:T(8,128)} %get-tuple-element.21, f32[16,4,128,1023]{3,0,2,1:T(8,128)} %get-tuple-element.20, ...), kind=kLoop, calls=%fused_computation.33 | loop fusion | flops 175636480 | bytes 138936320 | tf_op jit(solution)/shard_map/reduce_sum | solution.py:34
  371.8 46.2 %fusion.156 = (f32[16,4,128,1023]{3,0,2,1:T(8,128)}, f32[16,4,128,1023]{3,0,2,1:T(8,128)}) fusion(f32[16,4,128,1024]{3,0,2,1:T(8,128)} %get-tuple-element.7), kind=kLoop, calls=%fused_computation.161 | loop fusion | bytes 134086656 | tf_op jit(solution)/shard_map/jit(_roll_static)/slice | solution.py:38
  421.5 8.1 fusion.155
  429.6 27.8 %all-reduce.8.cloned.1.call-done = f32[4,128,1024]{2,1,0:T(8,128)} async-done(((f32[4,128,1024]{2,1,0:T(8,128)}), f32[4,128,1024]{2,1,0:T(8,128)}) %all-reduce.8.cloned.1.call-update) | async-done | bytes 2097168 | tf_op jit(solution)/shard_map/psum | solution.py:34
  457.4 70.9 %fusion = (f32[4,128,1024]{2,1,0:T(8,128)}, f32[16,4,128,1024]{3,0,2,1:T(8,128)}) fusion(f32[16]{0:T(128)S(1)} %copy-done.4, f32[16,4,128,1024]{3,0,2,1:T(8,128)} %get-tuple-element.7, f32[16,4,128,1]{3,0,2,1:T(8,128)} %get-tuple-element.13, f32[16,4,128,1023]{3,0,2,1:T(8,128)} %get-tuple-element.15, f32[16,4,128,1023]{3,0,2,1:T(8,128)} %get-tuple-element.14, ...), kind=kLoop, calls=%fused_computation.1 | loop fusion | flops 184025088 | bytes 138936384 | tf_op jit(solution)/shard_map/reduce_sum | solution.py:120
  528.3 16.6 %sine_negate_fusion = (f32[1024,1024]{1,0:T(8,128)S(1)}, f32[1024,1024]{1,0:T(8,128)S(1)}) fusion(), kind=kLoop, calls=%fused_computation.73 | loop fusion | flops 15728640 | bytes 8388608 | tf_op jit(solution)/shard_map/neg | solution.py:98
  552.3 9.3 copy.26
  561.5 9.8 %reduce-scatter.2.cloned.1.call-done = f32[4,32,1024]{2,1,0:T(8,128)} async-done(((f32[4,128,1024]{2,1,0:T(8,128)}), f32[4,32,1024]{2,1,0:T(8,128)}) %reduce-scatter.2.cloned.1.call-update) | async-done | bytes 524304 | tf_op jit(solution)/shard_map/reduce_scatter | solution.py:126
  571.3 11.6 %fusion.98 = f32[4,32,2,1024]{3,1,2,0:T(8,128)S(1)} fusion(f32[2,1024,1024,1]{2,1,0,3:T(8,128)} %bitcast.97, f32[4,32,1024]{2,1,0:T(8,128)} %reduce-scatter.2.cloned.1.call-done), kind=kOutput, calls=%fused_computation.95 | convolution fusion | flops 3221225472 | bytes 9961472 | tf_op jit(solution)/shard_map/dot_general | solution.py:99
  599.2 24.7 %all-to-all-done = f32[32,1,8192]{2,1,0:T(1,128)S(1)} async-done(((f32[32,1,8192]{2,1,0:T(1,128)}), f32[32,1,8192]{2,1,0:T(1,128)S(1)}, u32[]{:S(2)}, u32[]{:S(2)}) %all-to-all-start) | async-done | bytes 1048608 | tf_op jit(solution)/shard_map/all_to_all | solution.py:136
  643.2 18.9 %fusion.36 = f32[4,32,1024]{2,1,0:T(8,128)S(1)} fusion(s32[1024]{0:T(1024)S(1)} %fusion.108, f32[4,1024,2,32]{1,3,0,2:T(8,128)S(1)} %all_to_all.27), kind=kOutput, calls=%fused_computation.57 | convolution fusion | flops 1625292800 | bytes 1052672 | tf_op jit(solution)/shard_map/kq,pqc->pkc/dot_general | solution.py:59
  662.1 19.3 %fusion.38 = f32[4,32,1024]{2,1,0:T(8,128)S(1)} fusion(s32[1024]{0:T(1024)S(1)} %fusion.108, f32[4,1024,2,32]{1,3,0,2:T(8,128)S(1)} %all_to_all.27), kind=kOutput, calls=%fused_computation.59 | convolution fusion | flops 1625292800 | bytes 1052672 | tf_op jit(solution)/shard_map/kq,pqc->pkc/dot_general | solution.py:59
  681.4 19.0 %fusion.92 = f32[4,1024,32]{1,2,0:T(8,128)S(1)} fusion(f32[4,32,1024]{2,1,0:T(8,128)S(1)} %fusion.36, s32[1024]{0:T(1024)S(1)} %fusion.108, f32[4,1024,2,32]{1,3,0,2:T(8,128)S(1)} %all_to_all.27, f32[1024,32]{0,1:T(8,128)S(1)} %copy.29), kind=kOutput, calls=%fused_computation.90 | convolution fusion | flops 1625554944 | bytes 1708032 | tf_op jit(solution)/shard_map/kq,pqc->pkc/dot_general | solution.py:59
  700.5 18.5 %fusion.34 = f32[4,32,1024]{2,1,0:T(8,128)S(1)} fusion(f32[4,1024,32]{1,2,0:T(8,128)S(1)} %fusion.92, s32[1024]{0:T(1024)S(1)} %fusion.108), kind=kOutput, calls=%fused_computation.55 | convolution fusion | flops 1625292800 | bytes 1052672 | tf_op jit(solution)/shard_map/kq,pkc->pqc/dot_general | solution.py:69
  719.0 18.8 %fusion.95 = f32[4,1024,32]{1,2,0:T(8,128)S(1)} fusion(f32[4,32,1024]{2,1,0:T(8,128)S(1)} %fusion.38, s32[1024]{0:T(1024)S(1)} %fusion.108, f32[4,1024,2,32]{1,3,0,2:T(8,128)S(1)} %all_to_all.27, f32[1024,32]{0,1:T(8,128)S(1)} %copy.29), kind=kOutput, calls=%fused_computation.91 | convolution fusion | flops 1625554944 | bytes 1708032 | tf_op jit(solution)/shard_map/kq,pqc->pkc/dot_general | solution.py:59
  737.9 18.3 %fusion.32 = f32[4,32,1024]{2,1,0:T(8,128)S(1)} fusion(f32[4,1024,32]{1,2,0:T(8,128)S(1)} %fusion.95, s32[1024]{0:T(1024)S(1)} %fusion.108), kind=kOutput, calls=%fused_computation.53 | convolution fusion | flops 1625292800 | bytes 1052672 | tf_op jit(solution)/shard_map/kq,pkc->pqc/dot_general | solution.py:69
  756.2 18.5 %fusion.74 = f32[4,1024,1,32]{1,3,0,2:T(8,128)S(1)} fusion(f32[4,32,1024]{2,1,0:T(8,128)S(1)} %fusion.34, f32[4,1024,32]{1,2,0:T(8,128)S(1)} %fusion.95, s32[1024]{0:T(1024)S(1)} %fusion.108), kind=kOutput, calls=%fused_computation.84 | convolution fusion | flops 1625423872 | bytes 1576960 | tf_op jit(solution)/shard_map/kq,pkc->pqc/dot_general | solution.py:69
  774.7 18.1 %fusion.86 = f32[4,1024,1,32]{1,3,0,2:T(8,128)S(1)} fusion(f32[4,32,1024]{2,1,0:T(8,128)S(1)} %fusion.32, f32[4,1024,32]{1,2,0:T(8,128)S(1)} %fusion.92, s32[1024]{0:T(1024)S(1)} %fusion.108), kind=kOutput, calls=%fused_computation.88 | convolution fusion | flops 1625423872 | bytes 1576960 | tf_op jit(solution)/shard_map/kq,pkc->pqc/dot_general | solution.py:69
  800.4 29.8 %all_to_all.33 = f32[32,1,8192]{2,1,0:T(1,128)S(1)} all-to-all(f32[32,1,8192]{2,1,0:T(1,128)S(1)} %reshape.82), channel_id=1, replica_groups=mesh['grain'=4,'row'=8] {'grain','row'}, dimensions={0} | all-to-all | bytes 2097152 | tf_op jit(solution)/shard_map/all_to_all | solution.py:141
  847.3 8.9 fusion.89
  856.3 45.1 %all-gather.2.cloned.1.call-done = f32[4,128,1024]{2,1,0:T(8,128)} async-done(((f32[4,32,1024]{2,1,0:T(8,128)}), f32[4,128,1024]{2,1,0:T(8,128)}) %all-gather.2.cloned.1.call-update) | async-done | bytes 2097168 | tf_op jit(solution)/shard_map/all_gather | solution.py:143
  901.4 14.0 %multiply_subtract_fusion = f32[16,4,128,1024]{3,0,2,1:T(8,128)S(1)} fusion(f32[16,4,128,1024]{3,0,2,1:T(8,128)} %get-tuple-element.5, f32[4,128,1024]{2,1,0:T(8,128)} %all-gather.2.cloned.1.call-done, f32[16]{0:T(128)S(1)} %broadcast_multiply_fusion), kind=kLoop, calls=%fused_computation.32 | loop fusion | flops 25165824 | bytes 69206080 | tf_op jit(solution)/shard_map/sub | solution.py:145
  915.4 35.7 %copy.32 = f32[16,4,128,1024]{3,2,1,0:T(8,128)} copy(f32[16,4,128,1024]{3,0,2,1:T(8,128)S(1)} %multiply_subtract_fusion) | data formatting | bytes 67108864
  (55 shorter events, 79.3 us)
Async XLA Ops:
  7.2 138.4 %all-reduce.4.cloned.1.call-start = ((), (), s32[]{:S(2)}) async-start(), calls=%async_computation.3 | async-start | bytes 4194304 | tf_op jit(solution)/shard_map/psum | solution.py:34
  42.3 11.7 %copy-start = (f32[16,4,128,1024]{3,0,2,1:T(8,128)}, f32[16,4,128,1024]{3,0,2,1:T(8,128)S(1)}, u32[]{:S(2)}) copy-start(f32[16,4,128,1024]{3,0,2,1:T(8,128)S(1)} %get-tuple-element.23) | copy-start | bytes 100663296
  54.0 57.9 %collective-permute-start = (f32[16,4,1,1024]{3,0,2,1:T(8,128)S(1)}, f32[16,4,1,1024]{3,0,2,1:T(8,128)S(1)}, u32[]{:S(2)}, u32[]{:S(2)}) collective-permute-start(f32[16,4,1,1024]{3,0,2,1:T(8,128)S(1)} %get-tuple-element.24), channel_id=1, source_target_pairs={{1,0},{2,1},{3,2},{4,3},{5,4},{6,5},{7,6},{0,7},{9,8},{10,9},{11,1... | collective-permute-start | bytes 786440 | tf_op jit(solution)/shard_map/ppermute | solution.py:27
  57.4 54.5 %collective-permute-start.1 = (f32[16,4,1,1024]{3,0,2,1:T(8,128)S(1)}, f32[16,4,1,1024]{3,0,2,1:T(8,128)S(1)}, u32[]{:S(2)}, u32[]{:S(2)}) collective-permute-start(f32[16,4,1,1024]{3,0,2,1:T(8,128)S(1)} %get-tuple-element.25), channel_id=1, source_target_pairs={{0,1},{1,2},{2,3},{3,4},{4,5},{5,6},{6,7},{7,0},{8,9},{9,10},{10,1... | collective-permute-start | bytes 786440 | tf_op jit(solution)/shard_map/ppermute | solution.py:26
  57.5 244.1 %all-reduce.6.cloned.1.call-start = ((), (), s32[]{:S(2)}) async-start(), calls=%async_computation.4 | async-start | bytes 4194304 | tf_op jit(solution)/shard_map/psum | solution.py:34
  216.0 241.4 %all-reduce.8.cloned.1.call-start = ((), (), s32[]{:S(2)}) async-start(), calls=%async_computation.5 | async-start | bytes 4194304 | tf_op jit(solution)/shard_map/psum | solution.py:34
  263.0 10.3 %collective-permute-start.2 = (f32[16,4,1,1024]{3,0,2,1:T(8,128)S(1)}, f32[16,4,1,1024]{3,0,2,1:T(8,128)S(1)}, u32[]{:S(2)}, u32[]{:S(2)}) collective-permute-start(f32[16,4,1,1024]{3,0,2,1:T(8,128)S(1)} %get-tuple-element.16), channel_id=1, source_target_pairs={{1,0},{2,1},{3,2},{4,3},{5,4},{6,5},{7,6},{0,7},{9,8},{10,9},{11,1... | collective-permute-start | bytes 786440 | tf_op jit(solution)/shard_map/ppermute | solution.py:27
  264.9 8.5 collective-permute-start.3
  371.8 199.5 %reduce-scatter.2.cloned.1.call-start = ((), (), s32[]{:S(2)}) async-start(), calls=%async_computation.6 | async-start | bytes 2621440 | tf_op jit(solution)/shard_map/reduce_scatter | solution.py:126
  419.1 10.5 %collective-permute-start.4 = (f32[16,4,1,1024]{3,0,2,1:T(8,128)S(1)}, f32[16,4,1,1024]{3,0,2,1:T(8,128)S(1)}, u32[]{:S(2)}, u32[]{:S(2)}) collective-permute-start(f32[16,4,1,1024]{3,0,2,1:T(8,128)S(1)} %get-tuple-element.10), channel_id=1, source_target_pairs={{1,0},{2,1},{3,2},{4,3},{5,4},{6,5},{7,6},{0,7},{9,8},{10,9},{11,1... | collective-permute-start | bytes 786440 | tf_op jit(solution)/shard_map/ppermute | solution.py:27
  420.9 36.5 %copy-start.4 = (f32[16]{0:T(128)S(1)}, f32[16]{0:T(128)}, u32[]{:S(2)}) copy-start(f32[16]{0:T(128)} %param.4) | copy-start | bytes 196
  420.9 8.7 collective-permute-start.5
  545.0 1.9 copy-start.1
  545.0 3.3 copy-start.2
  593.8 30.2 %all-to-all-start = ((f32[32,1,8192]{2,1,0:T(1,128)}), f32[32,1,8192]{2,1,0:T(1,128)S(1)}, u32[]{:S(2)}, u32[]{:S(2)}) async-start(f32[32,1,8192]{2,1,0:T(1,128)} %reshape.80), calls=%async_computation.1 | async-start | bytes 2097152 | tf_op jit(solution)/shard_map/all_to_all | solution.py:136
  597.7 303.7 %all-gather.2.cloned.1.call-start = ((), (), s32[]{:S(2)}) async-start(), calls=%async_computation.7 | async-start | bytes 2621440 | tf_op jit(solution)/shard_map/all_gather | solution.py:143
  915.4 35.7 %copy-start.3 = (f32[4,128,1024]{2,1,0:T(8,128)S(1)}, f32[4,128,1024]{2,1,0:T(8,128)}, u32[]{:S(2)}) copy-start(f32[4,128,1024]{2,1,0:T(8,128)} %all-gather.2.cloned.1.call-done) | copy-start | bytes 6291460
Sparse Core Ops, SparseCore 0:
  57.6 87.9 all-reduce.3
  216.1 85.4 all-reduce.5
  371.9 85.4 all-reduce.7
  528.5 42.7 reduce-scatter.1
  856.4 44.9 all-gather.1
where the time goes:
time: 969 us; the launch traced here: 959 us
  other arithmetic  288 us (30%)
  local copies, waits for them, and re-layouts  275 us (28%)
  matrix products  170 us (18%)
  waiting for transfers between devices  169 us (17%)
  blocking collectives  29.8 us (3%)
  between operations  14.2 us (1%)
  starting transfers between devices  12.4 us (1%)
    reduce_sum x3, other arithmetic, advance(): totals = lax.psum(jnp.sum(center * center, axis=0), 'grain')  176 us
    slice x6, local copies, waits for them, and re-layouts, advance(): jnp.roll(center, 1, 3)  162 us
    psum x3, waiting for transfers between devices, advance(): totals = lax.psum(jnp.sum(center * center, axis=0), 'grain')  89.6 us
    dot_general x4, matrix products, forward_rows(): jnp.einsum('kq,pqc->pkc', matrix, values, precision=lax.Precision.HIGHEST...  76.1 us
    dot_general x4, matrix products, backward_rows(): jnp.einsum('kq,pkc->pqc', matrix, values, precision=lax.Precision.HIGHEST...  73.5 us
    unnamed x16, local copies, waits for them, and re-layouts  71.2 us
    reduce_sum x1, other arithmetic, local(): strain = jnp.sum(eigen_weight[:, None, None, None] * order * order, axis=0)  70.9 us
    all_gather x1, waiting for transfers between devices, local(): potential = lax.all_gather(potential, 'grain', axis=1, tiled=True)  45.1 us
  transfers between devices with their start and end apart: 12, of which 6 were waited for; matrix products, arithmetic and copies ran while one was open for 20% of the time, Pallas kernels for 0%

commit v1 on v0

v1 whole, which is shorter than its diff:
```python
import functools
import math

import jax
import jax.numpy as jnp
import numpy as np
from jax import lax
from jax.experimental import pallas as pl
from jax.experimental.pallas import tpu as pltpu
from jax.sharding import PartitionSpec as P

STEPS = 3

time_step = 0.1
alpha_coef = 1.0
beta_coef = 1.0
gamma_coef = 0.25
kappa_coef = 1.0
elastic_coef = 2.0

MESH = pl.DeviceIdType.MESH
HIGH = lax.Precision.HIGH
STRIP = 8


def steps_kernel(
    sizes, weight, order_in, order_out, strain_out,
    field, sums, send_up, send_down, in_up, in_down,
    edge_top, edge_bottom, halo_top, halo_bottom, above,
    load_sem, store_sem, strain_sem,
    up_send, up_recv, down_send, down_recv,
    top_send, top_recv, bottom_send, bottom_recv,
):
    chain, ring, grains, planes, rows, width = sizes
    z, r = lax.axis_index("grain"), lax.axis_index("row")
    before, after = lax.rem(r + ring - 1, ring), lax.rem(r + 1, ring)
    has_lower, has_upper = z > 0, z < chain - 1
    lower, upper = z - 1, z + 1
    lag_up = jnp.minimum(z, planes - 1)
    lag_down = jnp.minimum(chain - 1 - z, planes - 1)
    strips = rows // STRIP
    last = (STEPS + 1) * planes

    def load(p):
        return pltpu.make_async_copy(
            order_in.at[:, p], field.at[:, p, pl.ds(0, rows)], load_sem.at[p]
        )

    def store(p):
        return pltpu.make_async_copy(
            field.at[:, p, pl.ds(0, rows)], order_out.at[:, p], store_sem.at[p]
        )

    def up_copy(p, par):
        return pltpu.make_async_remote_copy(
            send_up.at[p], in_up.at[par, p], up_send.at[p], up_recv.at[par, p],
            device_id=(upper, r), device_id_type=MESH,
        )

    def down_copy(p, par):
        return pltpu.make_async_remote_copy(
            send_down.at[p], in_down.at[par, p], down_send.at[p], down_recv.at[par, p],
            device_id=(lower, r), device_id_type=MESH,
        )

    def top_copy(p, par):
        return pltpu.make_async_remote_copy(
            edge_top.at[p], halo_bottom.at[par, p], top_send.at[p], bottom_recv.at[par, p],
            device_id=(z, before), device_id_type=MESH,
        )

    def bottom_copy(p, par):
        return pltpu.make_async_remote_copy(
            edge_bottom.at[p], halo_top.at[par, p], bottom_send.at[p], top_recv.at[par, p],
            device_id=(z, after), device_id_type=MESH,
        )

    for p in range(planes):
        load(p).start()

    barrier = pltpu.get_barrier_semaphore()
    pl.semaphore_signal(barrier, inc=1, device_id=(z, before), device_id_type=MESH)
    pl.semaphore_signal(barrier, inc=1, device_id=(z, after), device_id_type=MESH)

    @pl.when(has_lower)
    def _():
        pl.semaphore_signal(barrier, inc=1, device_id=(lower, r), device_id_type=MESH)

    @pl.when(has_upper)
    def _():
        pl.semaphore_signal(barrier, inc=1, device_id=(upper, r), device_id_type=MESH)

    @pl.when(jnp.logical_not(has_lower))
    def _():
        in_up[...] = jnp.zeros_like(in_up)

    @pl.when(jnp.logical_not(has_upper))
    def _():
        in_down[...] = jnp.zeros_like(in_down)

    pl.semaphore_wait(barrier, 2 + has_lower.astype(jnp.int32) + has_upper.astype(jnp.int32))

    def send_edges(p, par):
        for g in range(grains):
            edge_top[p, pl.ds(g, 1), :] = field[g, p, pl.ds(0, 1), :]
            edge_bottom[p, pl.ds(g, 1), :] = field[g, p, pl.ds(rows - 1, 1), :]
        top_copy(p, par).start()
        bottom_copy(p, par).start()

    def first(p):
        load(p).wait()

        def strip(i, carry):
            at = pl.ds(pl.multiple_of(i * STRIP, STRIP), STRIP)
            total = jnp.zeros((STRIP, width), jnp.float32)
            for g in range(grains):
                value = field[g, p, at, :]
                total = total + value * value
            sums[p, at, :] = total
            return carry

        lax.fori_loop(0, strips, strip, 0)
        send_edges(p, 0)

    def advance(t, p, step):
        par = lax.rem(step, 2)
        bottom_copy(p, par).wait_recv()
        top_copy(p, par).wait_recv()
        above[...] = halo_top[par, p]
        for g in range(grains):
            field[g, p, pl.ds(rows, 1), :] = halo_bottom[par, p, pl.ds(g, 1), :]
        final = step == STEPS - 1
        row_id = lax.broadcasted_iota(jnp.int32, (STRIP, width), 0)
        scale = time_step * gamma_coef * 2.0
        base = 1.0 + time_step * alpha_coef - 4.0 * time_step * kappa_coef
        cube = time_step * beta_coef - scale
        spread = time_step * kappa_coef

        def strip(i, carry):
            start = pl.multiple_of(i * STRIP, STRIP)
            at = pl.ds(start, STRIP)
            total = sums[p, at, :] + (in_up[par, p, at, :] + in_down[par, p, at, :])
            shared = base - scale * total
            result = jnp.zeros((STRIP, width), jnp.float32)
            for g in range(grains):
                value = field[g, p, at, :]
                up_row = jnp.broadcast_to(above[pl.ds(g, 1), :], (STRIP, width))
                down_row = jnp.broadcast_to(
                    field[g, p, pl.ds(start + STRIP, 1), :], (STRIP, width)
                )
                above[pl.ds(g, 1), :] = value[STRIP - 1 :, :]
                up = jnp.where(row_id == 0, up_row, pltpu.roll(value, 1, 0))
                down = jnp.where(row_id == STRIP - 1, down_row, pltpu.roll(value, STRIP - 1, 0))
                around = (up + down) + (pltpu.roll(value, 1, 1) + pltpu.roll(value, width - 1, 1))
                fresh = value * (shared - cube * (value * value)) + spread * around
                field[g, p, at, :] = fresh
                factor = jnp.where(final, weight[g], 1.0)
                result = result + factor * (fresh * fresh)
            sums[p, at, :] = result
            return carry

        lax.fori_loop(0, strips, strip, 0)

        @pl.when(jnp.logical_not(final))
        def _():
            top_copy(p, par).wait_send()
            bottom_copy(p, par).wait_send()
            send_edges(p, 1 - par)

        @pl.when(final)
        def _():
            store(p).start()

    def add_into(target, p, incoming, par):
        def strip(i, carry):
            at = pl.ds(pl.multiple_of(i * STRIP, STRIP), STRIP)
            target[p, at, :] = incoming[par, p, at, :] + sums[p, at, :]
            return carry

        lax.fori_loop(0, strips, strip, 0)

    def forward_up(t):
        p, level = lax.rem(t, planes), t // planes
        par = lax.rem(level, 2)

        @pl.when(has_lower)
        def _():
            up_copy(p, par).wait_recv()

        @pl.when(has_upper)
        def _():
            @pl.when(level > 0)
            def _():
                up_copy(p, par).wait_send()

            add_into(send_up, p, in_up, par)
            up_copy(p, par).start()

    def forward_down(t):
        p, level = lax.rem(t, planes), t // planes
        par = lax.rem(level, 2)

        @pl.when(has_upper)
        def _():
            down_copy(p, par).wait_recv()

        @pl.when(has_lower)
        def _():
            @pl.when(level > 0)
            def _():
                down_copy(p, par).wait_send()

            add_into(send_down, p, in_down, par)
            down_copy(p, par).start()

    def slot(t, carry):
        p = lax.rem(t, planes)

        @pl.when(t < planes)
        def _():
            first(p)

        @pl.when(jnp.logical_and(t >= planes, t < last))
        def _():
            advance(t, p, t // planes - 1)

        up_t, down_t = t - lag_up, t - lag_down

        @pl.when(jnp.logical_and(up_t >= 0, up_t < last))
        def _():
            forward_up(up_t)

        @pl.when(jnp.logical_and(down_t >= 0, down_t < last))
        def _():
            forward_down(down_t)

        return carry

    lax.fori_loop(0, last + planes - 1, slot, 0)

    par = STEPS % 2
    for p in range(planes):
        def strip(i, carry):
            at = pl.ds(pl.multiple_of(i * STRIP, STRIP), STRIP)
            sums[p, at, :] = sums[p, at, :] + (in_up[par, p, at, :] + in_down[par, p, at, :])
            return carry

        lax.fori_loop(0, strips, strip, 0)
    out = pltpu.make_async_copy(sums, strain_out, strain_sem)
    out.start()
    for p in range(planes):
        top_copy(p, 0).wait_send()
        bottom_copy(p, 0).wait_send()
        store(p).wait()

        @pl.when(has_upper)
        def _():
            up_copy(p, par).wait_send()

        @pl.when(has_lower)
        def _():
            down_copy(p, par).wait_send()
    out.wait()


def run_steps(order, weight):
    chain, ring = lax.axis_size("grain"), lax.axis_size("row")
    grains, planes, rows, width = order.shape
    f32 = jnp.float32
    dma = pltpu.SemaphoreType.DMA
    plane = (planes, rows, width)
    edges = (planes, grains, width)
    return pl.pallas_call(
        functools.partial(steps_kernel, (chain, ring, grains, planes, rows, width)),
        out_shape=(
            jax.ShapeDtypeStruct(order.shape, f32),
            jax.ShapeDtypeStruct(plane, f32),
        ),
        in_specs=[pl.BlockSpec(memory_space=pltpu.SMEM), pl.BlockSpec(memory_space=pl.ANY)],
        out_specs=(pl.BlockSpec(memory_space=pl.ANY), pl.BlockSpec(memory_space=pl.ANY)),
        scratch_shapes=[
            pltpu.VMEM((grains, planes, rows + STRIP, width), f32),
            pltpu.VMEM(plane, f32),
            pltpu.VMEM(plane, f32),
            pltpu.VMEM(plane, f32),
            pltpu.VMEM((2,) + plane, f32),
            pltpu.VMEM((2,) + plane, f32),
            pltpu.VMEM(edges, f32),
            pltpu.VMEM(edges, f32),
            pltpu.VMEM((2,) + edges, f32),
            pltpu.VMEM((2,) + edges, f32),
            pltpu.VMEM((grains, width), f32),
            dma((planes,)),
            dma((planes,)),
            dma,
            dma((planes,)),
            dma((2, planes)),
            dma((planes,)),
            dma((2, planes)),
            dma((planes,)),
            dma((2, planes)),
            dma((planes,)),
            dma((2, planes)),
        ],
        compiler_params=pltpu.CompilerParams(
            collective_id=0, has_side_effects=True, vmem_limit_bytes=58 * 1024 * 1024
        ),
        cost_estimate=pl.CostEstimate(
            flops=60 * order.size, bytes_accessed=8 * order.size, transcendentals=0
        ),
    )(weight, order)


def row_tables(length, shares, ring):
    half = length // 2
    block = half // (shares * ring)
    places = np.arange(length)
    angle = 2.0 * math.pi / length * (np.outer(places, np.arange(half)) % length)
    cosine, sine = np.cos(angle), np.sin(angle)
    alternate = 1.0 - 2.0 * (places % 2)
    forward = np.stack([cosine, -sine], axis=1)
    forward[:, 1, 0] = alternate
    backward = 2.0 * np.stack([cosine, -sine], axis=1)
    backward[:, 0, 0] = 1.0
    backward[:, 1, 0] = alternate
    backward /= float(length) * float(length)

    def by_owner(table):
        table = table.reshape(length, 2, shares, ring, block).transpose(0, 2, 3, 1, 4)
        return table.reshape(length, shares, ring * 2 * block).astype(np.float32)

    return by_owner(forward).transpose(1, 0, 2).copy(), by_owner(backward).transpose(1, 2, 0).copy()


def column_table(length):
    places = np.arange(length)
    angle = 2.0 * math.pi / length * (np.outer(places, places) % length)
    return np.concatenate([np.cos(angle), np.sin(angle)], axis=0).astype(np.float32)


def flip_rows(x):
    return jnp.concatenate([x[:1], x[1:][::-1]], axis=0)


def even_green(green, start, block):
    length = green.shape[1]
    here = lax.dynamic_slice_in_dim(green, start, block, 1)
    tail = lax.dynamic_slice_in_dim(green, length - start - block, block, 1)
    head = lax.dynamic_slice_in_dim(green, (length - start) % length, 1, 1)
    mirror = jnp.concatenate([head, tail[:, ::-1][:, : block - 1]], axis=1)
    middle = green[:, length // 2 : length // 2 + 1]
    return 0.5 * (here + flip_rows(mirror)), 0.5 * (middle + flip_rows(middle))


def dot(a, b, dims):
    return lax.dot_general(
        a, b, (dims, ((), ())), precision=HIGH, preferred_element_type=jnp.float32
    )


def local(order_params, eigen_weight, green):
    order, strain = run_steps(order_params, eigen_weight)
    planes, rows, length = strain.shape
    chain, ring = lax.axis_size("grain"), lax.axis_size("row")
    z, r = lax.axis_index("grain"), lax.axis_index("row")
    shares = max(1, chain // planes)
    held = max(1, planes // chain)
    half = length // 2
    block = half // (shares * ring)
    forward, backward = row_tables(length, shares, ring)
    columns = jnp.asarray(column_table(length))
    part = z % shares
    start = (part * ring + r) * block
    even, middle = even_green(green, start, block)

    mine = lax.dynamic_slice_in_dim(strain, z // shares * held, held, 0).reshape(held * rows, length)
    pick = lambda table: lax.dynamic_index_in_dim(jnp.asarray(table), part, 0, keepdims=False)
    spectrum = dot(mine, pick(forward), ((1,), (0,)))
    spectrum = spectrum.reshape(held * rows, ring, 2 * block).transpose(1, 0, 2)
    spectrum = lax.all_to_all(spectrum, "row", split_axis=0, concat_axis=0, tiled=True)
    spectrum = spectrum.reshape(ring, held, rows, 2 * block).transpose(0, 2, 1, 3)
    spectrum = spectrum.reshape(ring * rows, held * 2 * block)

    product = dot(columns, spectrum, ((1,), (0,))).reshape(2, length, held, 2, block)
    cos_re, cos_im = product[0, :, :, 0], product[0, :, :, 1]
    sin_re, sin_im = product[1, :, :, 0], product[1, :, :, 1]
    packed = (start + jnp.arange(block) == 0)[None, None, :]
    g, m = even[:, None, :], middle[:, None, :]
    real, imag = g * (cos_re + sin_im), g * (cos_im - sin_re)
    x1 = jnp.where(packed, g * cos_re, real)
    x2 = jnp.where(packed, g * sin_re, -imag)
    x3 = jnp.where(packed, m * cos_im, imag)
    x4 = jnp.where(packed, m * sin_im, real)
    scaled = jnp.stack([jnp.stack([x1, x3], axis=2), jnp.stack([x2, x4], axis=2)], axis=0)
    scaled = scaled.reshape(2 * length, held * 2 * block)
    mixed = dot(columns, scaled, ((0,), (0,)))

    mixed = mixed.reshape(ring, rows, held, 2 * block).transpose(0, 2, 1, 3)
    mixed = mixed.reshape(ring, held * rows, 2 * block)
    mixed = lax.all_to_all(mixed, "row", split_axis=0, concat_axis=0, tiled=True)
    mixed = mixed.transpose(1, 0, 2).reshape(held * rows, ring * 2 * block)
    piece = dot(mixed, pick(backward), ((1,), (0,)))
    potential = lax.all_gather(piece, "grain", axis=0, tiled=True)
    if shares > 1:
        potential = jnp.sum(potential.reshape(planes, shares, rows, length), axis=1)
    potential = potential.reshape(planes, rows, length)
    factor = time_step * 2.0 * elastic_coef
    updated = order - factor * eigen_weight[:, None, None, None] * order * potential[None]
    return (updated, potential)


def solution(mesh):
    return jax.shard_map(
        local,
        mesh=mesh,
        in_specs=(P("grain", None, "row", None), P("grain"), P()),
        out_specs=(P("grain", None, "row", None), P(None, "row", None)),
        check_vma=False,
    )
```

time: 969 us -> 362 us (0.37)
  other arithmetic: 288 us -> 27.6 us
  local copies, waits for them, and re-layouts: 275 us -> 17.7 us
  Pallas kernels: 0 us -> 217 us
  matrix products: 170 us -> 25.2 us
  waiting for transfers between devices: 169 us -> 42.4 us
  blocking collectives: 29.8 us -> 13.4 us
    reduce_sum x4 -> x0, other arithmetic: 247 us -> none  [the longest x3 176 us: advance(): totals = lax.psum(jnp.sum(center * center, axis=0), 'grain')]
    pallas_call x0 -> x1, Pallas kernels: none -> 217 us  [run_steps(): pl.pallas_call(functools.partial(steps_kernel, (chain, ring, grains, plan...]
    slice x9 -> x6, local copies, waits for them, and re-layouts: 165 us -> 8.94 us  [the longest x2 4.44 us: even_green(): mirror = jnp.concatenate([head, tail[:, ::-1][:, :block - 1]], axis=1)]
    dot_general x10 -> x4, matrix products: 170 us -> 25.2 us  [dot(): lax.dot_general(a, b, (dims, ((), ())), precision=HIGH, preferred_element...]
    psum x3 -> x0, waiting for transfers between devices: 89.6 us -> none  [advance(): totals = lax.psum(jnp.sum(center * center, axis=0), 'grain')]
    unnamed x16 -> x19, local copies, waits for them, and re-layouts: 71.2 us -> 5.62 us
    all_to_all x1, waiting for transfers between devices: 24.7 us -> 0.01 us  [local(): lax.all_to_all(spectrum, 'row', split_axis=0, concat_axis=0, tiled=True)]
    all_to_all x4 -> x0, local copies, waits for them, and re-layouts: 17.8 us -> none  [the longest x3 11.1 us: local(): lax.all_to_all(forward, ('grain', 'row'), split_axis=3, concat_axis=1, ti...]
  transfers between devices with their start and end apart: 12 -> 2, of which waited for: 6 -> 1; matrix products, arithmetic and copies ran while one was open for 20% -> 4% of each run, Pallas kernels for 0% -> 0%
where the time goes in v1:
time: 362 us; the launch traced here: 361 us
  Pallas kernels  217 us (60%)
  waiting for transfers between devices  42.4 us (12%)
  other arithmetic  27.6 us (8%)
  matrix products  25.2 us (7%)
  local copies, waits for them, and re-layouts  17.7 us (5%)
  between operations  14.3 us (4%)
  blocking collectives  13.4 us (4%)
  starting transfers between devices  3.72 us (1%)
    pallas_call x1, Pallas kernels, run_steps(): pl.pallas_call(functools.partial(steps_kernel, (chain, ring, grains, plan...  217 us
    all_gather x1, waiting for transfers between devices, local(): potential = lax.all_gather(piece, 'grain', axis=0, tiled=True)  42.4 us
    sub x1, other arithmetic, local(): order - factor * eigen_weight[:, None, None, None] * order * potential[None]  26.1 us
    dot_general x4, matrix products, dot(): lax.dot_general(a, b, (dims, ((), ())), precision=HIGH, preferred_element...  25.2 us
    all_to_all x1, blocking collectives, local(): lax.all_to_all(mixed, 'row', split_axis=0, concat_axis=0, tiled=True)  13.4 us
  transfers between devices with their start and end apart: 2, of which 1 were waited for; matrix products, arithmetic and copies ran while one was open for 4% of the time, Pallas kernels for 0%

profile of v1, /device:TPU:0, one launch (start us, length us, event | category | flops | bytes accessed | tf_op | source)
XLA Modules:
  0.0 361.2 jit_solution(6490779138425964208)
XLA Ops:
  7.2 216.9 %shard_map.77 = (f32[16,4,128,1024]{3,2,1,0:T(8,128)}, f32[4,128,1024]{2,1,0:T(8,128)}) custom-call(f32[16]{0:T(128)} %weight.1, f32[16,4,128,1024]{3,2,1,0:T(8,128)} %order_in.1), custom_call_target="tpu_custom_call" | custom-call | flops 503316480 | bytes 67108864 | tf_op jit(solution)/shard_map/pallas_call | solution.py:273
  224.1 4.0 %convolution_bitcast_fusion = f32[8,128,128]{2,1,0:T(8,128)} fusion(f32[8,128,1024]{2,1,0:T(8,128)S(1)} %copy-done.1, f32[4,128,1024]{2,1,0:T(8,128)} %get-tuple-element.5, s32[]{:T(128)S(6)} %select_n.47), kind=kOutput, calls=%fused_computation.1 | convolution fusion | flops 805306368 | bytes 5242884 | tf_op jit(solution)/shard_map/dot_general | solution.py:356
  228.2 3.5 all-to-all-start
  231.7 0.2 all-gather.2.cloned.1.call-start
  231.9 1.2 constant_dynamic-slice_fusion
  233.2 1.4 fusion.9
  234.6 1.2 constant_dynamic-slice_fusion.2
  235.8 1.2 slice.42
  237.0 1.1 slice.43
  238.1 0.9 copy.38
  239.0 3.2 slice.36
  242.2 0.9 copy.35
  243.1 0.2 copy.43
  243.3 0.7 reverse.2
  244.1 0.2 copy.41
  244.3 0.2 copy.36
  244.6 0.7 reverse.1
  245.4 0.6 fusion.6
  246.1 7.6 %fusion.11 = f32[2048,128]{0,1:T(8,128)S(1)} fusion(f32[2048,1024]{1,0:T(8,128)} %constant.68.clone, f32[1024,128]{1,0:T(8,128)S(1)} %bitcast.85), kind=kOutput, calls=%fused_computation.34 | convolution fusion | flops 1610612736 | bytes 9961472 | tf_op jit(solution)/shard_map/dot_general | solution.py:356
  253.7 0.9 reshape.58
  254.6 0.8 fusion.10
  255.5 0.2 select_bitcast_fusion.2
  255.7 0.3 select_bitcast_fusion.1
  256.1 0.8 copy.31
  257.0 0.3 copy.45
  257.3 9.1 %fusion.12 = f32[1024,128]{1,0:T(8,128)S(1)} fusion(f32[2048,1024]{1,0:T(8,128)} %constant.68.clone, f32[2048,128]{0,1:T(8,128)S(1)} %bitcast.83), kind=kOutput, calls=%fused_computation.35 | convolution fusion | flops 1610612736 | bytes 9961472 | tf_op jit(solution)/shard_map/dot_general | solution.py:356
  266.5 0.2 copy.32
  266.7 13.4 %all_to_all.10 = f32[8,128,128]{1,2,0:T(8,128)S(1)} all-to-all(f32[8,128,128]{1,2,0:T(8,128)S(1)} %copy.32), channel_id=1, replica_groups=mesh['grain'=4,'row'=8] {'row'}, dimensions={0} | all-to-all | bytes 1048576 | tf_op jit(solution)/shard_map/all_to_all | solution.py:400
  280.1 4.3 %fusion.13 = f32[128,1024]{1,0:T(8,128)} fusion(f32[128,1024]{0,1:T(8,128)S(1)} %bitcast.87, f32[1024,1024]{1,0:T(8,128)} %constant.74), kind=kOutput, calls=%fused_computation.36 | convolution fusion | flops 805306368 | bytes 5242880 | tf_op jit(solution)/shard_map/dot_general | solution.py:356
  284.5 42.4 %all-gather.2.cloned.1.call-done = f32[512,1024]{1,0:T(8,128)} async-done(((f32[128,1024]{1,0:T(8,128)}), f32[512,1024]{1,0:T(8,128)}) %all-gather.2.cloned.1.call-update) | async-done | bytes 2097168 | tf_op jit(solution)/shard_map/all_gather | solution.py:403
  326.9 26.1 %multiply_subtract_fusion = f32[16,4,128,1024]{3,2,1,0:T(8,128)} fusion(f32[16,4,128,1024]{3,2,1,0:T(8,128)} %get-tuple-element.4, f32[4,128,1024]{2,1,0:T(8,128)} %bitcast.81, f32[16]{0:T(128)S(1)} %broadcast_multiply_fusion), kind=kLoop, calls=%fused_computation | loop fusion | flops 25165824 | bytes 69206080 | tf_op jit(solution)/shard_map/sub | solution.py:408
  353.0 1.3 copy.72
  (17 shorter events, 0.6 us)
Async XLA Ops:
  7.2 217.0 %copy-start.1 = (f32[8,128,1024]{2,1,0:T(8,128)S(1)}, f32[8,128,1024]{2,1,0:T(8,128)}, u32[]{:S(2)}) copy-start(f32[8,128,1024]{2,1,0:T(8,128)} %constant.73) | copy-start | bytes 12582916
  228.2 17.9 %all-to-all-start = ((f32[8,128,128]{2,1,0:T(8,128)}), f32[8,128,128]{2,1,0:T(8,128)S(1)}, u32[]{:S(2)}, u32[]{:S(2)}) async-start(f32[8,128,128]{2,1,0:T(8,128)} %convolution_bitcast_fusion), calls=%async_computation | async-start | bytes 1048576 | tf_op jit(solution)/shard_map/all_to_all | solution.py:380
  231.7 95.2 %all-gather.2.cloned.1.call-start = ((), (), s32[]{:S(2)}) async-start(), calls=%async_computation.2 | async-start | bytes 2621440 | tf_op jit(solution)/shard_map/all_gather | solution.py:403
  253.7 1.7 copy-start.2
  266.5 18.0 %copy-start.3 = (f32[16]{0:T(128)S(1)}, f32[16]{0:T(128)}, u32[]{:S(2)}) copy-start(f32[16]{0:T(128)} %weight.1) | copy-start | bytes 196
  326.9 26.2 %copy-start = (f32[512,1024]{1,0:T(8,128)S(1)}, f32[512,1024]{1,0:T(8,128)}, u32[]{:S(2)}) copy-start(f32[512,1024]{1,0:T(8,128)} %all-gather.2.cloned.1.call-done) | copy-start | bytes 6291460
Sparse Core Ops, SparseCore 0:
  284.6 42.2 all-gather.1

commit v2 on v1

--- a/solution.py
+++ b/solution.py
@@ -21,6 +21,8 @@
 MESH = pl.DeviceIdType.MESH
 HIGH = lax.Precision.HIGH
 STRIP = 8
+PIECES = 4
+GATHERS = 2
 
 
 def steps_kernel(
@@ -40,6 +42,17 @@
     lag_down = jnp.minimum(chain - 1 - z, planes - 1)
     strips = rows // STRIP
     last = (STEPS + 1) * planes
+    part = rows // PIECES
+    held, shares = max(1, planes // chain), max(1, chain // planes)
+
+    def plane_of(t):
+        i = lax.rem(t, planes)
+        odd = lax.rem(i, 2)
+        return (1 - odd) * (i // 2) + odd * (planes - 1 - i // 2)
+
+    def owners(p):
+        low = p // held * shares
+        return low, low + shares - 1
 
     def load(p):
         return pltpu.make_async_copy(
@@ -51,15 +64,17 @@
             field.at[:, p, pl.ds(0, rows)], order_out.at[:, p], store_sem.at[p]
         )
 
-    def up_copy(p, par):
+    def up_copy(p, par, c):
+        at = pl.ds(c * part, part)
         return pltpu.make_async_remote_copy(
-            send_up.at[p], in_up.at[par, p], up_send.at[p], up_recv.at[par, p],
+            send_up.at[p, at], in_up.at[par, p, at], up_send.at[p, c], up_recv.at[par, p, c],
             device_id=(upper, r), device_id_type=MESH,
         )
 
-    def down_copy(p, par):
+    def down_copy(p, par, c):
+        at = pl.ds(c * part, part)
         return pltpu.make_async_remote_copy(
-            send_down.at[p], in_down.at[par, p], down_send.at[p], down_recv.at[par, p],
+            send_down.at[p, at], in_down.at[par, p, at], down_send.at[p, c], down_recv.at[par, p, c],
             device_id=(lower, r), device_id_type=MESH,
         )
 
@@ -75,8 +90,8 @@
             device_id=(z, after), device_id_type=MESH,
         )
 
-    for p in range(planes):
-        load(p).start()
+    for i in range(planes):
+        load(plane_of(i)).start()
 
     barrier = pltpu.get_barrier_semaphore()
     pl.semaphore_signal(barrier, inc=1, device_id=(z, before), device_id_type=MESH)
@@ -171,95 +186,98 @@
         def _():
             store(p).start()
 
-    def add_into(target, p, incoming, par):
+    def add_into(target, p, incoming, par, c):
+        def strip(i, carry):
+            at = pl.ds(pl.multiple_of(c * part + i * STRIP, STRIP), STRIP)
+            target[p, at, :] = incoming[par, p, at, :] + sums[p, at, :]
+            return carry
+
+        lax.fori_loop(0, part // STRIP, strip, 0)
+
+    def forward(t, copy, incoming, target, takes, gives):
+        p, level = plane_of(t), t // planes
+        par = lax.rem(level, 2)
+        for c in range(PIECES):
+            @pl.when(takes(p, level))
+            def _():
+                copy(p, par, c).wait_recv()
+
+            @pl.when(gives(p, level))
+            def _():
+                @pl.when(level > 0)
+                def _():
+                    copy(p, par, c).wait_send()
+
+                add_into(target, p, incoming, par, c)
+                copy(p, par, c).start()
+
+    def takes_up(p, level):
+        return jnp.logical_and(has_lower, jnp.logical_or(level < STEPS, z <= owners(p)[1]))
+
+    def gives_up(p, level):
+        return jnp.logical_and(has_upper, jnp.logical_or(level < STEPS, z < owners(p)[1]))
+
+    def takes_down(p, level):
+        return jnp.logical_and(has_upper, jnp.logical_or(level < STEPS, z >= owners(p)[0]))
+
+    def gives_down(p, level):
+        return jnp.logical_and(has_lower, jnp.logical_or(level < STEPS, z > owners(p)[0]))
+
+    def forward_up(t):
+        forward(t, up_copy, in_up, send_up, takes_up, gives_up)
+
+    def forward_down(t):
+        forward(t, down_copy, in_down, send_down, takes_down, gives_down)
+
+    def slot(t, carry):
+        p = plane_of(t)
+
+        @pl.when(t < planes)
+        def _():
+            first(p)
+
+        @pl.when(jnp.logical_and(t >= planes, t < last))
+        def _():
+            advance(t, p, t // planes - 1)
+
+        up_t, down_t = t - lag_up, t - lag_down
+
+        @pl.when(jnp.logical_and(up_t >= 0, up_t < last))
+        def _():
+            forward_up(up_t)
+
+        @pl.when(jnp.logical_and(down_t >= 0, down_t < last))
+        def _():
+            forward_down(down_t)
+
+        return carry
+
+    lax.fori_loop(0, last + planes - 1, slot, 0)
+
+    par = STEPS % 2
+    mine = z // shares * held
+    for k in range(held):
         def strip(i, carry):
             at = pl.ds(pl.multiple_of(i * STRIP, STRIP), STRIP)
-            target[p, at, :] = incoming[par, p, at, :] + sums[p, at, :]
-            return carry
-
-        lax.fori_loop(0, strips, strip, 0)
-
-    def forward_up(t):
-        p, level = lax.rem(t, planes), t // planes
-        par = lax.rem(level, 2)
-
-        @pl.when(has_lower)
-        def _():
-            up_copy(p, par).wait_recv()
-
-        @pl.when(has_upper)
-        def _():
-            @pl.when(level > 0)
-            def _():
-                up_copy(p, par).wait_send()
-
-            add_into(send_up, p, in_up, par)
-            up_copy(p, par).start()
-
-    def forward_down(t):
-        p, level = lax.rem(t, planes), t // planes
-        par = lax.rem(level, 2)
-
-        @pl.when(has_upper)
-        def _():
-            down_copy(p, par).wait_recv()
-
-        @pl.when(has_lower)
-        def _():
-            @pl.when(level > 0)
-            def _():
-                down_copy(p, par).wait_send()
-
-            add_into(send_down, p, in_down, par)
-            down_copy(p, par).start()
-
-    def slot(t, carry):
-        p = lax.rem(t, planes)
-
-        @pl.when(t < planes)
-        def _():
-            first(p)
-
-        @pl.when(jnp.logical_and(t >= planes, t < last))
-        def _():
-            advance(t, p, t // planes - 1)
-
-        up_t, down_t = t - lag_up, t - lag_down
-
-        @pl.when(jnp.logical_and(up_t >= 0, up_t < last))
-        def _():
-            forward_up(up_t)
-
-        @pl.when(jnp.logical_and(down_t >= 0, down_t < last))
-        def _():
-            forward_down(down_t)
-
-        return carry
-
-    lax.fori_loop(0, last + planes - 1, slot, 0)
-
-    par = STEPS % 2
-    for p in range(planes):
-        def strip(i, carry):
-            at = pl.ds(pl.multiple_of(i * STRIP, STRIP), STRIP)
+            p = mine + k
             sums[p, at, :] = sums[p, at, :] + (in_up[par, p, at, :] + in_down[par, p, at, :])
             return carry
 
         lax.fori_loop(0, strips, strip, 0)
-    out = pltpu.make_async_copy(sums, strain_out, strain_sem)
+    out = pltpu.make_async_copy(sums.at[pl.ds(mine, held)], strain_out, strain_sem)
     out.start()
     for p in range(planes):
         top_copy(p, 0).wait_send()
         bottom_copy(p, 0).wait_send()
         store(p).wait()
-
-        @pl.when(has_upper)
-        def _():
-            up_copy(p, par).wait_send()
-
-        @pl.when(has_lower)
-        def _():
-            down_copy(p, par).wait_send()
+        for c in range(PIECES):
+            @pl.when(has_upper)
+            def _():
+                up_copy(p, par, c).wait_send()
+
+            @pl.when(has_lower)
+            def _():
+                down_copy(p, par, c).wait_send()
     out.wait()
 
 
@@ -274,7 +292,7 @@
         functools.partial(steps_kernel, (chain, ring, grains, planes, rows, width)),
         out_shape=(
             jax.ShapeDtypeStruct(order.shape, f32),
-            jax.ShapeDtypeStruct(plane, f32),
+            jax.ShapeDtypeStruct((max(1, planes // chain), rows, width), f32),
         ),
         in_specs=[pl.BlockSpec(memory_space=pltpu.SMEM), pl.BlockSpec(memory_space=pl.ANY)],
         out_specs=(pl.BlockSpec(memory_space=pl.ANY), pl.BlockSpec(memory_space=pl.ANY)),
@@ -293,10 +311,10 @@
             dma((planes,)),
             dma((planes,)),
             dma,
-            dma((planes,)),
-            dma((2, planes)),
-            dma((planes,)),
-            dma((2, planes)),
+            dma((planes, PIECES)),
+            dma((2, planes, PIECES)),
+            dma((planes, PIECES)),
+            dma((2, planes, PIECES)),
             dma((planes,)),
             dma((2, planes)),
             dma((planes,)),
@@ -358,13 +376,46 @@
     )
 
 
+def update_kernel(grains, weight, order, potential, *rest):
+    out = rest[-1]
+    factor = time_step * 2.0 * elastic_coef
+    for i in range(grains):
+        scale = factor * weight[pl.program_id(0) * grains + i]
+        value = order[i]
+        out[i] = value - scale * value * potential[...]
+
+
+def update_rows(k, weight, order, potential, filled):
+    grains, planes, rows, width = order.shape
+    part = potential.shape[1]
+    group = math.gcd(grains, 2)
+    block = pl.BlockSpec((group, planes, part, width), lambda g: (g, 0, k, 0))
+    whole = pl.BlockSpec((planes, part, width), lambda g: (0, 0, 0))
+    extra = [] if filled is None else [filled]
+    return pl.pallas_call(
+        functools.partial(update_kernel, group),
+        grid=(grains // group,),
+        out_shape=jax.ShapeDtypeStruct(order.shape, order.dtype),
+        in_specs=[pl.BlockSpec(memory_space=pltpu.SMEM), block, whole]
+        + [pl.BlockSpec(memory_space=pl.ANY)] * len(extra),
+        out_specs=block,
+        input_output_aliases={3: 0} if extra else {},
+        cost_estimate=pl.CostEstimate(
+            flops=3 * order.size * part // rows,
+            bytes_accessed=8 * order.size * part // rows,
+            transcendentals=0,
+        ),
+        compiler_params=pltpu.CompilerParams(vmem_limit_bytes=32 * 1024 * 1024),
+    )(weight, order, potential, *extra)
+
+
 def local(order_params, eigen_weight, green):
     order, strain = run_steps(order_params, eigen_weight)
-    planes, rows, length = strain.shape
+    planes = order.shape[1]
+    held, rows, length = strain.shape
     chain, ring = lax.axis_size("grain"), lax.axis_size("row")
     z, r = lax.axis_index("grain"), lax.axis_index("row")
     shares = max(1, chain // planes)
-    held = max(1, planes // chain)
     half = length // 2
     block = half // (shares * ring)
     forward, backward = row_tables(length, shares, ring)
@@ -373,7 +424,7 @@
     start = (part * ring + r) * block
     even, middle = even_green(green, start, block)
 
-    mine = lax.dynamic_slice_in_dim(strain, z // shares * held, held, 0).reshape(held * rows, length)
+    mine = strain.reshape(held * rows, length)
     pick = lambda table: lax.dynamic_index_in_dim(jnp.asarray(table), part, 0, keepdims=False)
     spectrum = dot(mine, pick(forward), ((1,), (0,)))
     spectrum = spectrum.reshape(held * rows, ring, 2 * block).transpose(1, 0, 2)
@@ -400,13 +451,18 @@
     mixed = lax.all_to_all(mixed, "row", split_axis=0, concat_axis=0, tiled=True)
     mixed = mixed.transpose(1, 0, 2).reshape(held * rows, ring * 2 * block)
     piece = dot(mixed, pick(backward), ((1,), (0,)))
-    potential = lax.all_gather(piece, "grain", axis=0, tiled=True)
-    if shares > 1:
-        potential = jnp.sum(potential.reshape(planes, shares, rows, length), axis=1)
-    potential = potential.reshape(planes, rows, length)
-    factor = time_step * 2.0 * elastic_coef
-    updated = order - factor * eigen_weight[:, None, None, None] * order * potential[None]
-    return (updated, potential)
+    piece = piece.reshape(held, rows, length)
+    updated, gathered = None, []
+    part = rows // GATHERS
+    for k in range(GATHERS):
+        potential = lax.all_gather(
+            piece[:, k * part : (k + 1) * part], "grain", axis=0, tiled=True
+        )
+        if shares > 1:
+            potential = jnp.sum(potential.reshape(planes, shares, part, length), axis=1)
+        gathered.append(potential)
+        updated = update_rows(k, eigen_weight, order, potential, updated)
+    return (updated, jnp.concatenate(gathered, axis=1))
 
 
 def solution(mesh):

time: 362 us -> 335 us (0.925)
  other arithmetic: 27.6 us -> 4.38 us
    pallas_call x1, Pallas kernels: 217 us -> 186 us  [run_steps(): pl.pallas_call(functools.partial(steps_kernel, (chain, ring, grains, plan...]
    pallas_call x0 -> x2, Pallas kernels: none -> 28.6 us  [update_rows(): pl.pallas_call(functools.partial(update_kernel, group), grid=(grains // g...]
    sub x1 -> x0, other arithmetic: 26.1 us -> none  [local(): order - factor * eigen_weight[:, None, None, None] * order * potential[None]]
    all_gather x1 -> x2, waiting for transfers between devices: 42.4 us -> 45.2 us  [local(): lax.all_gather(piece[:, k * part:(k + 1) * part], 'grain', axis=0, tiled=...]
  transfers between devices with their start and end apart: 2 -> 3, of which waited for: 1 -> 2; matrix products, arithmetic and copies ran while one was open for 4% -> 3% of each run, Pallas kernels for 0% -> 4%
where the time goes in v2:
time: 335 us; the launch traced here: 334 us
  Pallas kernels  214 us (64%)
  waiting for transfers between devices  45.9 us (14%)
  matrix products  24.4 us (7%)
  between operations  14.2 us (4%)
  local copies, waits for them, and re-layouts  14.1 us (4%)
  blocking collectives  13.4 us (4%)
  other arithmetic  4.38 us (1%)
  starting transfers between devices  3.76 us (1%)
    pallas_call x1, Pallas kernels, run_steps(): pl.pallas_call(functools.partial(steps_kernel, (chain, ring, grains, plan...  186 us
    all_gather x2, waiting for transfers between devices, local(): lax.all_gather(piece[:, k * part:(k + 1) * part], 'grain', axis=0, tiled=...  45.2 us
    pallas_call x2, Pallas kernels, update_rows(): pl.pallas_call(functools.partial(update_kernel, group), grid=(grains // g...  28.6 us
    dot_general x4, matrix products, dot(): lax.dot_general(a, b, (dims, ((), ())), precision=HIGH, preferred_element...  24.4 us
    all_to_all x1, blocking collectives, local(): lax.all_to_all(mixed, 'row', split_axis=0, concat_axis=0, tiled=True)  13.4 us
  transfers between devices with their start and end apart: 3, of which 2 were waited for; matrix products, arithmetic and copies ran while one was open for 3% of the time, Pallas kernels for 4%

profile of v2, /device:TPU:0, one launch (start us, length us, event | category | flops | bytes accessed | tf_op | source)
XLA Modules:
  0.0 334.5 jit_solution(15773542298658559300)
XLA Ops:
  7.2 185.7 %shard_map.77 = (f32[16,4,128,1024]{3,2,1,0:T(8,128)}, f32[1,128,1024]{2,1,0:T(8,128)}) custom-call(f32[16]{0:T(128)} %weight.5, f32[16,4,128,1024]{3,2,1,0:T(8,128)} %order_in.1), custom_call_target="tpu_custom_call" | custom-call | flops 503316480 | bytes 67108864 | tf_op jit(solution)/shard_map/pallas_call | solution.py:291
  192.9 4.0 %convolution_bitcast_fusion.1 = f32[8,128,128]{2,1,0:T(8,128)} fusion(f32[8,128,1024]{2,1,0:T(8,128)S(1)} %copy-done.4, f32[1,128,1024]{2,1,0:T(8,128)} %get-tuple-element.5), kind=kOutput, calls=%fused_computation.2 | convolution fusion | flops 805306368 | bytes 5242880 | tf_op jit(solution)/shard_map/dot_general | solution.py:374
  196.9 3.5 %all-to-all-start = ((f32[8,128,128]{2,1,0:T(8,128)}), f32[8,128,128]{2,1,0:T(8,128)S(1)}, u32[]{:S(2)}, u32[]{:S(2)}) async-start(f32[8,128,128]{2,1,0:T(8,128)} %convolution_bitcast_fusion.1), calls=%async_computation | async-start | bytes 1048576 | tf_op jit(solution)/shard_map/all_to_all | solution.py:431
  200.4 0.2 all-gather.5.cloned.1.call-start
  200.7 1.1 slice.49
  201.8 1.2 slice.48
  203.0 1.4 fusion.9
  204.6 1.2 constant_dynamic-slice_fusion
  205.8 0.2 copy.39
  206.0 0.3 slice.42
  206.5 0.7 reverse.1
  207.3 1.2 constant_dynamic-slice_fusion.2
  209.1 0.7 reverse.2
  209.9 0.7 fusion.7
  210.6 7.6 %fusion.12 = f32[2048,128]{0,1:T(8,128)S(1)} fusion(f32[2048,1024]{1,0:T(8,128)} %constant.54.clone, f32[1024,128]{1,0:T(8,128)S(1)} %bitcast.84), kind=kOutput, calls=%fused_computation.34 | convolution fusion | flops 1610612736 | bytes 9961472 | tf_op jit(solution)/shard_map/dot_general | solution.py:374
  218.2 0.9 reshape.57
  219.1 0.8 fusion.10
  219.9 0.2 select_bitcast_fusion.2
  220.2 0.3 select_bitcast_fusion.1
  220.7 0.8 copy.32
  221.5 0.3 copy.46
  221.8 9.1 %fusion.13 = f32[1024,128]{1,0:T(8,128)S(1)} fusion(f32[2048,1024]{1,0:T(8,128)} %constant.54.clone, f32[2048,128]{0,1:T(8,128)S(1)} %bitcast.82), kind=kOutput, calls=%fused_computation.35 | convolution fusion | flops 1610612736 | bytes 9961472 | tf_op jit(solution)/shard_map/dot_general | solution.py:374
  231.2 13.4 %all_to_all.10 = f32[8,128,128]{1,2,0:T(8,128)S(1)} all-to-all(f32[8,128,128]{1,2,0:T(8,128)S(1)} %copy.33), channel_id=1, replica_groups=mesh['grain'=4,'row'=8] {'row'}, dimensions={0} | all-to-all | bytes 1048576 | tf_op jit(solution)/shard_map/all_to_all | solution.py:451
  244.6 3.5 %convolution_bitcast_fusion = f32[1,128,1024]{2,1,0:T(8,128)S(1)} fusion(f32[128,1024]{0,1:T(8,128)S(1)} %bitcast.86, f32[1024,1024]{1,0:T(8,128)} %constant.60), kind=kOutput, calls=%fused_computation.1 | convolution fusion | flops 805306368 | bytes 5242880 | tf_op jit(solution)/shard_map/dot_general | solution.py:374
  248.2 0.8 fusion.11
  249.1 0.7 all-gather.3.cloned.1.call-update
  249.8 31.8 %all-gather.5.cloned.1.call-done.potential = f32[4,64,1024]{2,1,0:T(8,128)} async-done(((f32[1,64,1024]{2,1,0:T(8,128)}), f32[4,64,1024]{2,1,0:T(8,128)}) %all-gather.5.cloned.1.call-update) | async-done | bytes 1048592 | tf_op jit(solution)/shard_map/all_gather | solution.py:458
  281.6 1.2 copy-done
  282.8 14.4 %shard_map.78.rest_0_ = f32[16,4,128,1024]{3,2,1,0:T(8,128)} custom-call(f32[16]{0:T(128)S(1)} %copy-done.3, f32[16,4,128,1024]{3,2,1,0:T(8,128)} %get-tuple-element.4.order, f32[4,64,1024]{2,1,0:T(8,128)S(1)} %copy-done), custom_call_target="tpu_custom_call" | custom-call | flops 12582912 | bytes 33554432 | tf_op jit(solution)/shard_map/pallas_call | solution.py:395
  297.2 13.4 %all-gather.3.cloned.1.call-done.potential = f32[4,64,1024]{2,1,0:T(8,128)} async-done(((f32[1,64,1024]{2,1,0:T(8,128)}), f32[4,64,1024]{2,1,0:T(8,128)}) %all-gather.3.cloned.1.call-update) | async-done | bytes 1048592 | tf_op jit(solution)/shard_map/all_gather | solution.py:458
  310.6 2.8 pad_maximum_fusion
  313.4 14.2 %shard_map.79 = f32[16,4,128,1024]{3,2,1,0:T(8,128)} custom-call(f32[16]{0:T(128)S(1)} %copy-done.3, f32[16,4,128,1024]{3,2,1,0:T(8,128)} %get-tuple-element.4.order, f32[4,64,1024]{2,1,0:T(8,128)S(1)} %copy-done.2, f32[16,4,128,1024]{3,2,1,0:T(8,128)} %shard_map.78.rest_0_), custom_call_target="tpu_custom_call", output_to_operand_aliasing={{}: (3, {})} | custom-call | flops 12582912 | bytes 33554432 | tf_op jit(solution)/shard_map/pallas_call | solution.py:395
  (23 shorter events, 1.5 us)
Async XLA Ops:
  7.2 185.7 %copy-start.4 = (f32[8,128,1024]{2,1,0:T(8,128)S(1)}, f32[8,128,1024]{2,1,0:T(8,128)}, u32[]{:S(2)}) copy-start(f32[8,128,1024]{2,1,0:T(8,128)} %constant.59) | copy-start | bytes 12582916
  196.9 13.7 %all-to-all-start = ((f32[8,128,128]{2,1,0:T(8,128)}), f32[8,128,128]{2,1,0:T(8,128)S(1)}, u32[]{:S(2)}, u32[]{:S(2)}) async-start(f32[8,128,128]{2,1,0:T(8,128)} %convolution_bitcast_fusion.1), calls=%async_computation | async-start | bytes 1048576 | tf_op jit(solution)/shard_map/all_to_all | solution.py:431
  200.4 81.1 %all-gather.5.cloned.1.call-start = ((), (), s32[]{:S(2)}) async-start(), calls=%async_computation.3 | async-start | bytes 1310720 | tf_op jit(solution)/shard_map/all_gather | solution.py:458
  231.2 50.4 %copy-start.3 = (f32[16]{0:T(128)S(1)}, f32[16]{0:T(128)}, u32[]{:S(2)}) copy-start(f32[16]{0:T(128)} %weight.5) | copy-start | bytes 196
  249.0 61.6 %all-gather.3.cloned.1.call-start = ((), (), s32[]{:S(2)}) async-start(), calls=%async_computation.2 | async-start | bytes 1310720 | tf_op jit(solution)/shard_map/all_gather | solution.py:458
  281.6 1.2 copy-start
  282.8 27.8 %copy-start.1 = (f32[4,64,1024]{2,1,0:T(8,128)S(1)}, f32[4,64,1024]{2,1,0:T(8,128)}, u32[]{:S(2)}) copy-start(f32[4,64,1024]{2,1,0:T(8,128)} %all-gather.5.cloned.1.call-done.potential) | copy-start | bytes 3145732
  310.6 2.8 copy-start.2
Sparse Core Ops, SparseCore 0:
  249.2 32.3 all-gather.4
  283.1 27.4 all-gather.2

commit v3 on v2

--- a/solution.py
+++ b/solution.py
@@ -22,7 +22,6 @@
 HIGH = lax.Precision.HIGH
 STRIP = 8
 PIECES = 4
-GATHERS = 2
 
 
 def steps_kernel(
@@ -376,39 +375,6 @@
     )
 
 
-def update_kernel(grains, weight, order, potential, *rest):
-    out = rest[-1]
-    factor = time_step * 2.0 * elastic_coef
-    for i in range(grains):
-        scale = factor * weight[pl.program_id(0) * grains + i]
-        value = order[i]
-        out[i] = value - scale * value * potential[...]
-
-
-def update_rows(k, weight, order, potential, filled):
-    grains, planes, rows, width = order.shape
-    part = potential.shape[1]
-    group = math.gcd(grains, 2)
-    block = pl.BlockSpec((group, planes, part, width), lambda g: (g, 0, k, 0))
-    whole = pl.BlockSpec((planes, part, width), lambda g: (0, 0, 0))
-    extra = [] if filled is None else [filled]
-    return pl.pallas_call(
-        functools.partial(update_kernel, group),
-        grid=(grains // group,),
-        out_shape=jax.ShapeDtypeStruct(order.shape, order.dtype),
-        in_specs=[pl.BlockSpec(memory_space=pltpu.SMEM), block, whole]
-        + [pl.BlockSpec(memory_space=pl.ANY)] * len(extra),
-        out_specs=block,
-        input_output_aliases={3: 0} if extra else {},
-        cost_estimate=pl.CostEstimate(
-            flops=3 * order.size * part // rows,
-            bytes_accessed=8 * order.size * part // rows,
-            transcendentals=0,
-        ),
-        compiler_params=pltpu.CompilerParams(vmem_limit_bytes=32 * 1024 * 1024),
-    )(weight, order, potential, *extra)
-
-
 def local(order_params, eigen_weight, green):
     order, strain = run_steps(order_params, eigen_weight)
     planes = order.shape[1]
@@ -451,18 +417,13 @@
     mixed = lax.all_to_all(mixed, "row", split_axis=0, concat_axis=0, tiled=True)
     mixed = mixed.transpose(1, 0, 2).reshape(held * rows, ring * 2 * block)
     piece = dot(mixed, pick(backward), ((1,), (0,)))
-    piece = piece.reshape(held, rows, length)
-    updated, gathered = None, []
-    part = rows // GATHERS
-    for k in range(GATHERS):
-        potential = lax.all_gather(
-            piece[:, k * part : (k + 1) * part], "grain", axis=0, tiled=True
-        )
-        if shares > 1:
-            potential = jnp.sum(potential.reshape(planes, shares, part, length), axis=1)
-        gathered.append(potential)
-        updated = update_rows(k, eigen_weight, order, potential, updated)
-    return (updated, jnp.concatenate(gathered, axis=1))
+    potential = lax.all_gather(piece, "grain", axis=0, tiled=True)
+    if shares > 1:
+        potential = jnp.sum(potential.reshape(planes, shares, rows, length), axis=1)
+    potential = potential.reshape(planes, rows, length)
+    factor = time_step * 2.0 * elastic_coef
+    updated = order - factor * eigen_weight[:, None, None, None] * order * potential[None]
+    return (updated, potential)
 
 
 def solution(mesh):

time: 335 us -> 339 us (1.012)
  Pallas kernels: 214 us -> 186 us
  other arithmetic: 4.38 us -> 27.6 us
  waiting for transfers between devices: 45.9 us -> 50.5 us
  local copies, waits for them, and re-layouts: 14.1 us -> 17.7 us
    pallas_call x2 -> x0, Pallas kernels: 28.6 us -> none  [update_rows(): pl.pallas_call(functools.partial(update_kernel, group), grid=(grains // g...]
    sub x0 -> x1, other arithmetic: none -> 26.1 us  [local(): order - factor * eigen_weight[:, None, None, None] * order * potential[None]]
    all_gather x2 -> x1, waiting for transfers between devices: 45.2 us -> 50.5 us  [local(): potential = lax.all_gather(piece, 'grain', axis=0, tiled=True)]
  transfers between devices with their start and end apart: 3 -> 2, of which waited for: 2 -> 1; matrix products, arithmetic and copies ran while one was open for 3% -> 4% of each run, Pallas kernels for 4% -> 0%
where the time goes in v3:
time: 339 us; the launch traced here: 338 us
  Pallas kernels  186 us (55%)
  waiting for transfers between devices  50.5 us (15%)
  other arithmetic  27.6 us (8%)
  matrix products  25.2 us (7%)
  local copies, waits for them, and re-layouts  17.7 us (5%)
  between operations  14.2 us (4%)
  blocking collectives  13.4 us (4%)
  starting transfers between devices  3.72 us (1%)
    pallas_call x1, Pallas kernels, run_steps(): pl.pallas_call(functools.partial(steps_kernel, (chain, ring, grains, plan...  186 us
    all_gather x1, waiting for transfers between devices, local(): potential = lax.all_gather(piece, 'grain', axis=0, tiled=True)  50.5 us
    sub x1, other arithmetic, local(): order - factor * eigen_weight[:, None, None, None] * order * potential[None]  26.1 us
    dot_general x4, matrix products, dot(): lax.dot_general(a, b, (dims, ((), ())), precision=HIGH, preferred_element...  25.2 us
    all_to_all x1, blocking collectives, local(): lax.all_to_all(mixed, 'row', split_axis=0, concat_axis=0, tiled=True)  13.4 us
  transfers between devices with their start and end apart: 2, of which 1 were waited for; matrix products, arithmetic and copies ran while one was open for 4% of the time, Pallas kernels for 0%

profile of v3, /device:TPU:0, one launch (start us, length us, event | category | flops | bytes accessed | tf_op | source)
XLA Modules:
  0.0 338.1 jit_solution(5693992368051897168)
XLA Ops:
  7.2 185.7 %shard_map.77 = (f32[16,4,128,1024]{3,2,1,0:T(8,128)}, f32[1,128,1024]{2,1,0:T(8,128)}) custom-call(f32[16]{0:T(128)} %weight.1, f32[16,4,128,1024]{3,2,1,0:T(8,128)} %order_in.1), custom_call_target="tpu_custom_call" | custom-call | flops 503316480 | bytes 67108864 | tf_op jit(solution)/shard_map/pallas_call | solution.py:290
  192.9 4.0 %convolution_bitcast_fusion = f32[8,128,128]{2,1,0:T(8,128)} fusion(f32[8,128,1024]{2,1,0:T(8,128)S(1)} %copy-done.1, f32[1,128,1024]{2,1,0:T(8,128)} %get-tuple-element.5), kind=kOutput, calls=%fused_computation.1 | convolution fusion | flops 805306368 | bytes 5242880 | tf_op jit(solution)/shard_map/dot_general | solution.py:373
  196.9 3.5 %all-to-all-start = ((f32[8,128,128]{2,1,0:T(8,128)}), f32[8,128,128]{2,1,0:T(8,128)S(1)}, u32[]{:S(2)}, u32[]{:S(2)}) async-start(f32[8,128,128]{2,1,0:T(8,128)} %convolution_bitcast_fusion), calls=%async_computation | async-start | bytes 1048576 | tf_op jit(solution)/shard_map/all_to_all | solution.py:397
  200.4 0.2 all-gather.2.cloned.1.call-start
  200.7 1.2 constant_dynamic-slice_fusion
  201.9 1.4 fusion.9
  203.3 1.2 constant_dynamic-slice_fusion.2
  204.6 1.2 slice.42
  205.8 1.1 slice.43
  206.9 0.9 copy.38
  207.8 3.2 slice.36
  211.0 0.9 copy.35
  211.9 0.2 copy.43
  212.1 0.7 reverse.2
  212.8 0.2 copy.41
  213.0 0.2 copy.36
  213.4 0.7 reverse.1
  214.2 0.6 fusion.7
  214.8 7.6 %fusion.11 = f32[2048,128]{0,1:T(8,128)S(1)} fusion(f32[2048,1024]{1,0:T(8,128)} %constant.56.clone, f32[1024,128]{1,0:T(8,128)S(1)} %bitcast.85), kind=kOutput, calls=%fused_computation.33 | convolution fusion | flops 1610612736 | bytes 9961472 | tf_op jit(solution)/shard_map/dot_general | solution.py:373
  222.5 0.9 reshape.58
  223.4 0.8 fusion.10
  224.2 0.2 select_bitcast_fusion.2
  224.4 0.3 select_bitcast_fusion.1
  224.9 0.8 copy.31
  225.7 0.3 copy.45
  226.1 9.1 %fusion.12 = f32[1024,128]{1,0:T(8,128)S(1)} fusion(f32[2048,1024]{1,0:T(8,128)} %constant.56.clone, f32[2048,128]{0,1:T(8,128)S(1)} %bitcast.83), kind=kOutput, calls=%fused_computation.34 | convolution fusion | flops 1610612736 | bytes 9961472 | tf_op jit(solution)/shard_map/dot_general | solution.py:373
  235.2 0.2 copy.32
  235.4 13.4 %all_to_all.10 = f32[8,128,128]{1,2,0:T(8,128)S(1)} all-to-all(f32[8,128,128]{1,2,0:T(8,128)S(1)} %copy.32), channel_id=1, replica_groups=mesh['grain'=4,'row'=8] {'row'}, dimensions={0} | all-to-all | bytes 1048576 | tf_op jit(solution)/shard_map/all_to_all | solution.py:417
  248.9 4.3 %fusion.13 = f32[128,1024]{1,0:T(8,128)} fusion(f32[128,1024]{0,1:T(8,128)S(1)} %bitcast.87, f32[1024,1024]{1,0:T(8,128)} %constant.62), kind=kOutput, calls=%fused_computation.35 | convolution fusion | flops 805306368 | bytes 5242880 | tf_op jit(solution)/shard_map/dot_general | solution.py:373
  253.2 50.5 %all-gather.2.cloned.1.call-done = f32[512,1024]{1,0:T(8,128)} async-done(((f32[128,1024]{1,0:T(8,128)}), f32[512,1024]{1,0:T(8,128)}) %all-gather.2.cloned.1.call-update) | async-done | bytes 2097168 | tf_op jit(solution)/shard_map/all_gather | solution.py:420
  303.8 26.1 %multiply_subtract_fusion = f32[16,4,128,1024]{3,2,1,0:T(8,128)} fusion(f32[16,4,128,1024]{3,2,1,0:T(8,128)} %get-tuple-element.4, f32[4,128,1024]{2,1,0:T(8,128)} %bitcast.81, f32[16]{0:T(128)S(1)} %broadcast_multiply_fusion), kind=kLoop, calls=%fused_computation | loop fusion | flops 25165824 | bytes 69206080 | tf_op jit(solution)/shard_map/sub | solution.py:425
  329.9 1.3 copy.72
  (17 shorter events, 0.6 us)
Async XLA Ops:
  7.2 185.7 %copy-start.1 = (f32[8,128,1024]{2,1,0:T(8,128)S(1)}, f32[8,128,1024]{2,1,0:T(8,128)}, u32[]{:S(2)}) copy-start(f32[8,128,1024]{2,1,0:T(8,128)} %constant.61) | copy-start | bytes 12582916
  196.9 17.9 %all-to-all-start = ((f32[8,128,128]{2,1,0:T(8,128)}), f32[8,128,128]{2,1,0:T(8,128)S(1)}, u32[]{:S(2)}, u32[]{:S(2)}) async-start(f32[8,128,128]{2,1,0:T(8,128)} %convolution_bitcast_fusion), calls=%async_computation | async-start | bytes 1048576 | tf_op jit(solution)/shard_map/all_to_all | solution.py:397
  200.4 103.3 %all-gather.2.cloned.1.call-start = ((), (), s32[]{:S(2)}) async-start(), calls=%async_computation.2 | async-start | bytes 2621440 | tf_op jit(solution)/shard_map/all_gather | solution.py:420
  212.8 11.4 %copy-start.2 = (f32[1024,64]{0,1:T(8,128)S(1)}, f32[1024,64]{0,1:T(8,128)}, u32[]{:S(2)}) copy-start(f32[1024,64]{0,1:T(8,128)} %copy.35) | copy-start | bytes 786436
  226.1 27.2 %copy-start.3 = (f32[16]{0:T(128)S(1)}, f32[16]{0:T(128)}, u32[]{:S(2)}) copy-start(f32[16]{0:T(128)} %weight.1) | copy-start | bytes 196
  303.8 26.2 %copy-start = (f32[512,1024]{1,0:T(8,128)S(1)}, f32[512,1024]{1,0:T(8,128)}, u32[]{:S(2)}) copy-start(f32[512,1024]{1,0:T(8,128)} %all-gather.2.cloned.1.call-done) | copy-start | bytes 6291460
Sparse Core Ops, SparseCore 0:
  253.3 50.3 all-gather.1
